TPU v7x, 256 devices: a whole 4x4x8 slice. The times are simulated.
256 devices in a mesh: rows: 64 (over x, z, core), cols: 4 (over y).
Axes of the slice: x: 4, y: 4, z: 8, core: 2. Of those that a mesh axis runs over, the one named last changes fastest.
Arguments:
- kernel: float32 [16384, 16384], P('rows', 'cols'), may hold values from 0 to 2, as said below
- row_block: int32 [256], P('rows'), may hold values from 0 to 255, as said below
- panel_order: int32 [2], replicated, may hold values from 0 to 63, as said below
- samples: float32 [16384, 512], P('rows', 'cols'), may hold values from -6 to 6
Outputs:
- trailing: float32 [16384, 16384], P('rows', 'cols')
- factor: float32 [16384, 512], P('rows')
- solved: float32 [512, 512], P(None, 'cols')
- reduced_samples: float32 [16384, 512], P('rows', 'cols')
Inputs may be any that keep to these rules, and one draw needn't show every extreme that they name: `row_block`: the stored row blocks of rows index i (stored blocks i * 4 to (i + 1) * 4 - 1) hold the global row blocks i + t * 64, t = 0 .. 3, each once, in some order. `panel_order`: the entries are distinct, and one of them is 63. `kernel`: in global row order the matrix is symmetric and positive definite, its smallest eigenvalue 0.25 or more.
All inputs are finite; a program needn't handle non-finite values.
Results may differ from a plain program's by a relative error of at most 0.0003.
Values sent between devices are 32-bit elements; how exact they have to be, the bound alone decides.
No kernel may reach another device: no remote copies, remote signals or barrier semaphores. Data moves between devices by JAX's collectives and lax.ppermute only.
A program may use at most 128 MiB of HBM per device.

v0:
```python
import jax
import jax.numpy as jnp
from jax import lax
from jax.sharding import PartitionSpec as P

PW = 256
PANELS = 2
EXACT = lax.Precision.HIGHEST


def broadcast(block, axis, owner):
    block = jnp.where(lax.axis_index(axis) == owner, block, jnp.zeros_like(block))
    return lax.psum(block, axis)


def times_transposed(left_side, right_side):
    return lax.dot_general(
        left_side,
        right_side,
        (((1,), (1,)), ((), ())),
        precision=EXACT,
        preferred_element_type=jnp.float32,
    )


def matmul_plain(left_side, right_side):
    return jnp.dot(left_side, right_side, precision=EXACT, preferred_element_type=jnp.float32)


def stored_order(array, restore, blocks_here):
    width_here = array.shape[1]
    return jnp.take(array.reshape(blocks_here, -1, width_here), restore, axis=0).reshape(
        array.shape
    )


def on_device(kernel, row_block, panel_order, samples):
    rows_count = lax.axis_size("rows")
    cols_count = lax.axis_size("cols")
    cols_place = lax.axis_index("cols")
    blocks_here = row_block.shape[0]
    local_rows, local_cols = kernel.shape
    block_rows = local_rows // blocks_here
    per_panel = PW // block_rows
    share = blocks_here // cols_count
    right_cols = samples.shape[1]
    ranking = jnp.argsort(row_block)
    restore = jnp.argsort(ranking)
    sorted_blocks = jnp.take(row_block, ranking)
    trailing_work = jnp.take(
        kernel.reshape(blocks_here, block_rows, local_cols), ranking, axis=0
    ).reshape(local_rows, local_cols)
    right_side = jnp.take(
        samples.reshape(blocks_here, block_rows, right_cols), ranking, axis=0
    ).reshape(local_rows, right_cols)
    identity = jnp.eye(PW, dtype=jnp.float32)
    factors = []
    solutions = []
    for panel_step in range(PANELS):
        panel_start = panel_order[panel_step] * PW
        column_owner = panel_start // local_cols
        offset = panel_start - column_owner * local_cols
        own_columns = lax.dynamic_slice_in_dim(trailing_work, offset, PW, 1)
        columns = broadcast(own_columns, "cols", column_owner)
        first_block = panel_order[panel_step] * per_panel
        wanted = first_block + jnp.arange(per_panel, dtype=jnp.int32)
        chooser = (wanted[:, None] == sorted_blocks[None, :]).astype(jnp.float32)
        diag_part = jnp.einsum(
            "ot,trp->orp", chooser, columns.reshape(blocks_here, block_rows, PW), precision=EXACT
        ).reshape(PW, PW)
        right_part = jnp.einsum(
            "ot,trp->orp",
            chooser,
            right_side.reshape(blocks_here, block_rows, right_cols),
            precision=EXACT,
        ).reshape(PW, right_cols)
        diagonal, panel_right = lax.psum((diag_part, right_part), "rows")
        lower_factor = jnp.linalg.cholesky(diagonal)
        inverse = jax.scipy.linalg.solve_triangular(lower_factor, identity, lower=True)
        factor_own = times_transposed(columns, inverse)
        solved_now = matmul_plain(inverse, panel_right)
        right_side = right_side - matmul_plain(factor_own, solved_now)
        my_piece = lax.dynamic_slice_in_dim(
            factor_own, cols_place * share * block_rows, share * block_rows, 0
        )
        spread = times_transposed(factor_own, lax.all_gather(my_piece, "rows", axis=0, tiled=True))
        update = (
            spread.reshape(local_rows, rows_count, share, block_rows)
            .transpose(0, 2, 1, 3)
            .reshape(local_rows, local_cols)
        )
        trailing_work = trailing_work - update
        factors.append(factor_own)
        solutions.append(solved_now)
    factor_all = jnp.concatenate(factors, 1)
    return (
        stored_order(trailing_work, restore, blocks_here),
        stored_order(factor_all, restore, blocks_here),
        jnp.concatenate(solutions, 0),
        stored_order(right_side, restore, blocks_here),
    )


def solution(mesh):
    in_specs = (P("rows", "cols"), P("rows"), P(), P("rows", "cols"))
    out_specs = (P("rows", "cols"), P("rows", None), P(None, "cols"), P("rows", "cols"))
    return jax.shard_map(
        on_device, mesh=mesh, in_specs=in_specs, out_specs=out_specs, check_vma=False
    )
```

profile of v0, /device:TPU:1, one launch (start us, length us, event | category | flops | bytes accessed | tf_op | source)
XLA Modules:
  0.0 816.9 jit_solution(4630192233342211881)
XLA Ops:
  7.2 1.3 fusion.51
  9.2 1.4 sort.31
  10.6 1.3 gather_fusion
  11.9 5.0 gather_fusion.2
  16.9 2.7 broadcast_select_fusion.1
  19.6 2.0 copy-done.2
  21.6 0.7 dynamic-slice_select_fusion.1
  24.0 0.7 copy.24
  24.7 46.3 %all-reduce.8.cloned.1.call-done = f32[256,256]{1,0:T(8,128)} async-done(((f32[256,256]{1,0:T(8,128)}), f32[256,256]{1,0:T(8,128)}) %all-reduce.8.cloned.1.call-update) | async-done | bytes 262160 | tf_op jit(solution)/shard_map/psum | solution.py:13
  71.0 1.5 fusion.4
  72.6 0.8 copy.17
  73.6 183.5 %all-reduce.14.cloned.1.call-done = (f32[256,256]{0,1:T(8,128)}, f32[256,128]{1,0:T(8,128)}) async-done(((f32[256,256]{0,1:T(8,128)}, f32[256,128]{1,0:T(8,128)}), (f32[256,256]{0,1:T(8,128)}, f32[256,128]{1,0:T(8,128)})) %all-reduce.14.cloned.1.call-update) | async-done | bytes 393232 | tf_op jit(solution)/shard_map/psum | solution.py:77
  257.1 1.1 copy.18
  258.2 1.0 fusion.1
  259.2 11.7 %cholesky.130 = f32[128,128]{1,0:T(8,128)S(1)} custom-call(f32[128,128]{1,0:T(8,128)S(1)} %cholesky.194), custom_call_target="Cholesky" | custom-call | tf_op jit(solution)/shard_map/jit(cholesky)/cholesky | solution.py:78
  271.0 9.8 %custom-call.13 = f32[1,128,128]{1,2,0:T(8,128)S(1)} custom-call(f32[1,128,128]{2,1,0:T(8,128)S(1)} %get-tuple-element.61), custom_call_target="InvertDiagBlocksLowerTriangular" | custom-call | tf_op jit(solution)/shard_map/jit(cholesky)/cholesky | solution.py:78
  281.3 11.7 %cholesky.147 = f32[128,128]{1,0:T(8,128)S(1)} custom-call(f32[128,128]{1,0:T(8,128)S(1)} %convolution_subtract_fusion.7), custom_call_target="Cholesky" | custom-call | tf_op jit(solution)/shard_map/jit(cholesky)/cholesky | solution.py:78
  293.1 0.6 compare_reduce_fusion.2
  295.1 4.5 while.4
  296.2 1.4 bitcast_dynamic-update-slice_fusion.4
  298.2 1.4 bitcast_dynamic-update-slice_fusion.4
  299.6 19.7 %custom-call.14 = f32[2,128,128]{1,2,0:T(8,128)S(1)} custom-call(f32[2,128,128]{2,1,0:T(8,128)S(1)} %get-tuple-element.26), custom_call_target="InvertDiagBlocksLowerTriangular" | custom-call | tf_op jit(solution)/shard_map/jit(_solve_triangular)/triangular_solve | solution.py:79
  323.1 78.1 %all-gather.3.cloned.1.call-done = f32[4096,256]{1,0:T(8,128)} async-done(((f32[64,256]{1,0:T(8,128)}), f32[4096,256]{1,0:T(8,128)}) %all-gather.3.cloned.1.call-update) | async-done | bytes 4194320 | tf_op jit(solution)/shard_map/all_gather | solution.py:86
  401.1 11.4 %convolution_subtract_fusion.1 = f32[256,4096]{1,0:T(8,128)S(1)} fusion(f32[256,4096]{1,0:T(8,128)} %bitcast.108, f32[256,256]{1,0:T(8,128)S(1)} %fusion.10, f32[4096,256]{1,0:T(8,128)} %all-gather.3.cloned.1.call-done), kind=kOutput, calls=%fused_computation.11 | convolution fusion | flops 3222274048 | bytes 12845056 | tf_op jit(solution)/shard_map/dot_general | solution.py:17
  412.6 2.0 copy-done.1
  414.6 0.7 dynamic-slice_select_fusion
  416.1 0.7 copy.26
  416.8 40.3 %all-reduce.10.cloned.1.call-done = f32[256,256]{1,0:T(8,128)} async-done(((f32[256,256]{1,0:T(8,128)}), f32[256,256]{1,0:T(8,128)}) %all-reduce.10.cloned.1.call-update) | async-done | bytes 262160 | tf_op jit(solution)/shard_map/psum | solution.py:13
  457.1 1.5 fusion.2
  458.7 0.8 copy.21
  459.8 183.3 %all-reduce.12.cloned.1.call-done = (f32[256,256]{0,1:T(8,128)}, f32[256,128]{1,0:T(8,128)}) async-done(((f32[256,256]{0,1:T(8,128)}, f32[256,128]{1,0:T(8,128)}), (f32[256,256]{0,1:T(8,128)}, f32[256,128]{1,0:T(8,128)})) %all-reduce.12.cloned.1.call-update) | async-done | bytes 393232 | tf_op jit(solution)/shard_map/psum | solution.py:77
  643.0 1.1 copy.22
  644.2 1.0 fusion
  645.2 11.7 %cholesky.164 = f32[128,128]{1,0:T(8,128)S(1)} custom-call(f32[128,128]{1,0:T(8,128)S(1)} %cholesky.197), custom_call_target="Cholesky" | custom-call | tf_op jit(solution)/shard_map/jit(cholesky)/cholesky | solution.py:78
  656.9 9.8 %custom-call.15 = f32[1,128,128]{1,2,0:T(8,128)S(1)} custom-call(f32[1,128,128]{2,1,0:T(8,128)S(1)} %get-tuple-element.57), custom_call_target="InvertDiagBlocksLowerTriangular" | custom-call | tf_op jit(solution)/shard_map/jit(cholesky)/cholesky | solution.py:78
  667.2 11.7 %cholesky.181 = f32[128,128]{1,0:T(8,128)S(1)} custom-call(f32[128,128]{1,0:T(8,128)S(1)} %convolution_subtract_fusion.6), custom_call_target="Cholesky" | custom-call | tf_op jit(solution)/shard_map/jit(cholesky)/cholesky | solution.py:78
  681.6 4.2 while.5
  682.4 1.4 bitcast_dynamic-update-slice_fusion.5
  684.4 1.4 bitcast_dynamic-update-slice_fusion.5
  685.8 19.7 %custom-call.16 = f32[2,128,128]{1,2,0:T(8,128)S(1)} custom-call(f32[2,128,128]{2,1,0:T(8,128)S(1)} %get-tuple-element.27), custom_call_target="InvertDiagBlocksLowerTriangular" | custom-call | tf_op jit(solution)/shard_map/jit(_solve_triangular)/triangular_solve | solution.py:79
  707.5 0.7 sort.32
  710.4 0.7 pad_maximum_fusion.3
  711.2 0.7 broadcast_select_fusion.2
  711.9 0.9 bitcast_select_fusion
  712.8 74.6 %all-gather.5.cloned.1.call-done = f32[4096,256]{1,0:T(8,128)} async-done(((f32[64,256]{1,0:T(8,128)}), f32[4096,256]{1,0:T(8,128)}) %all-gather.5.cloned.1.call-update) | async-done | bytes 4194320 | tf_op jit(solution)/shard_map/all_gather | solution.py:86
  787.4 12.7 %convolution_subtract_fusion = f32[256,4096]{1,0:T(8,128)} fusion(f32[256,4096]{1,0:T(8,128)} %copy-done.1, f32[256,256]{1,0:T(8,128)S(1)} %fusion.8, f32[4096,256]{1,0:T(8,128)} %all-gather.5.cloned.1.call-done), kind=kOutput, calls=%fused_computation.10 | convolution fusion | flops 3222274048 | bytes 12845056 | tf_op jit(solution)/shard_map/dot_general | solution.py:17
  800.1 4.9 gather_fusion.3
  805.0 4.8 broadcast_select_fusion
  (88 shorter events, 13.7 us)
Async XLA Ops:
  7.2 15.9 %copy-start = (f32[256,128]{1,0:T(8,128)S(1)}, f32[256,128]{1,0:T(8,128)}, u32[]{:S(2)}) copy-start(f32[256,128]{1,0:T(8,128)} %param.14) | copy-start | bytes 393220
  7.2 63.8 %all-reduce.8.cloned.1.call-start = ((), (), s32[]{:S(2)}) async-start(), calls=%async_computation | async-start | bytes 524288 | tf_op jit(solution)/shard_map/psum | solution.py:13
  19.6 2.0 copy-start.2
  22.4 234.8 %all-reduce.14.cloned.1.call-start = ((), (), s32[]{:S(2)}) async-start(), calls=%async_computation.5 | async-start | bytes 786432 | tf_op jit(solution)/shard_map/psum | solution.py:77
  71.0 249.2 %copy-start.3 = (f32[256,256]{1,0:T(8,128)S(1)}, f32[256,256]{1,0:T(8,128)}, u32[]{:S(2)}) copy-start(f32[256,256]{1,0:T(8,128)} %all-reduce.8.cloned.1.call-done) | copy-start | bytes 786436
  73.5 327.7 %all-gather.3.cloned.1.call-start = ((), (), s32[]{:S(2)}) async-start(), calls=%async_computation.1 | async-start | bytes 4259840 | tf_op jit(solution)/shard_map/all_gather | solution.py:86
  257.1 65.6 %copy-start.5 = (f32[256,128]{1,0:T(8,128)S(1)}, f32[256,128]{1,0:T(8,128)}, u32[]{:S(2)}) copy-start(f32[256,128]{1,0:T(8,128)} %get-tuple-element.47) | copy-start | bytes 393220
  321.3 135.8 %all-reduce.10.cloned.1.call-start = ((), (), s32[]{:S(2)}) async-start(), calls=%async_computation.2 | async-start | bytes 524288 | tf_op jit(solution)/shard_map/psum | solution.py:13
  412.6 2.0 copy-start.1
  415.3 227.7 %all-reduce.12.cloned.1.call-start = ((), (), s32[]{:S(2)}) async-start(), calls=%async_computation.4 | async-start | bytes 786432 | tf_op jit(solution)/shard_map/psum | solution.py:77
  457.1 249.3 %copy-start.4 = (f32[256,256]{1,0:T(8,128)S(1)}, f32[256,256]{1,0:T(8,128)}, u32[]{:S(2)}) copy-start(f32[256,256]{1,0:T(8,128)} %all-reduce.10.cloned.1.call-done) | copy-start | bytes 786436
  459.5 327.8 %all-gather.5.cloned.1.call-start = ((), (), s32[]{:S(2)}) async-start(), calls=%async_computation.3 | async-start | bytes 4259840 | tf_op jit(solution)/shard_map/all_gather | solution.py:86
  643.0 65.4 %copy-start.6 = (f32[256,128]{1,0:T(8,128)S(1)}, f32[256,128]{1,0:T(8,128)}, u32[]{:S(2)}) copy-start(f32[256,128]{1,0:T(8,128)} %get-tuple-element.45) | copy-start | bytes 393220
Sparse Core Ops, SparseCore 0:
  22.5 48.4 all-reduce.7
  75.5 181.5 all-reduce.13
  321.4 79.7 all-gather.2
  415.5 41.5 all-reduce.9
  461.4 181.5 all-reduce.11
  707.6 79.7 all-gather.4
where the time goes:
time: 826 us; the launch traced here: 817 us
  waiting for transfers between devices  606 us (73%)
  other arithmetic  124 us (15%)
  local copies, waits for them, and re-layouts  33.1 us (4%)
  matrix products  32.9 us (4%)
  between operations  20 us (2%)
    psum x2, waiting for transfers between devices, on_device(): diagonal, panel_right = lax.psum((diag_part, right_part), 'rows')  367 us
    all_gather x2, waiting for transfers between devices, on_device(): lax.all_gather(my_piece, 'rows', axis=0, tiled=True)  153 us
    psum x2, waiting for transfers between devices, broadcast(): return lax.psum(block, axis)  86.6 us
    another operation x13, other arithmetic, on_device(): lower_factor = jnp.linalg.cholesky(diagonal)  68.5 us
    another operation x5, other arithmetic, on_device(): jax.scipy.linalg.solve_triangular(lower_factor, identity, lower=True)  39.4 us
    dot_general x4, matrix products, times_transposed(): lax.dot_general(left_side, right_side, (((1,), (1,)), ((), ())), precisio...  25 us
  transfers between devices with their start and end apart: 6, of which 6 were waited for; matrix products, arithmetic and copies ran while one was open for 1% of the time, Pallas kernels for 0%

commit v1 on v0

--- a/solution.py
+++ b/solution.py
@@ -10,7 +10,7 @@
 
 def broadcast(block, axis, owner):
     block = jnp.where(lax.axis_index(axis) == owner, block, jnp.zeros_like(block))
-    return lax.psum(block, axis)
+    return jnp.sum(lax.all_gather(block, axis), axis=0)
 
 
 def times_transposed(left_side, right_side):

time: 826 us -> 787 us (0.953)
  waiting for transfers between devices: 606 us -> 565 us
    psum x2 -> x0, waiting for transfers between devices: 86.6 us -> none  [broadcast(): return lax.psum(block, axis)]
    all_gather x0 -> x2, waiting for transfers between devices: none -> 48.1 us  [broadcast(): return jnp.sum(lax.all_gather(block, axis), axis=0)]
    another operation x13 -> x14, other arithmetic: 68.5 us -> 69.2 us  [on_device(): lower_factor = jnp.linalg.cholesky(diagonal)]
where the time goes in v1:
time: 787 us; the launch traced here: 777 us
  waiting for transfers between devices  565 us (72%)
  other arithmetic  127 us (16%)
  local copies, waits for them, and re-layouts  33.1 us (4%)
  matrix products  30.9 us (4%)
  between operations  20 us (3%)
    psum x2, waiting for transfers between devices, on_device(): diagonal, panel_right = lax.psum((diag_part, right_part), 'rows')  363 us
    all_gather x2, waiting for transfers between devices, on_device(): lax.all_gather(my_piece, 'rows', axis=0, tiled=True)  154 us
    another operation x14, other arithmetic, on_device(): lower_factor = jnp.linalg.cholesky(diagonal)  69.2 us
    all_gather x2, waiting for transfers between devices, broadcast(): return jnp.sum(lax.all_gather(block, axis), axis=0)  48.1 us
    another operation x5, other arithmetic, on_device(): jax.scipy.linalg.solve_triangular(lower_factor, identity, lower=True)  39.4 us
    dot_general x4, matrix products, times_transposed(): lax.dot_general(left_side, right_side, (((1,), (1,)), ((), ())), precisio...  25 us
  transfers between devices with their start and end apart: 6, of which 6 were waited for; matrix products, arithmetic and copies ran while one was open for 1% of the time, Pallas kernels for 0%

profile of v1, /device:TPU:1, one launch (start us, length us, event | category | flops | bytes accessed | tf_op | source)
XLA Modules:
  0.0 777.2 jit_solution(17165101057978029686)
XLA Ops:
  7.2 1.3 fusion.51
  9.2 1.4 sort.31
  10.6 1.3 gather_fusion
  12.6 5.0 gather_fusion.2
  17.6 2.7 broadcast_select_fusion.1
  20.3 2.0 copy-done.2
  22.3 0.7 dynamic-slice_select_fusion.1
  24.1 0.7 copy.23
  24.8 27.9 %all-gather.11.cloned.1.call-done = f32[1024,256]{1,0:T(8,128)} async-done(((f32[256,256]{1,0:T(8,128)}), f32[1024,256]{1,0:T(8,128)}) %all-gather.11.cloned.1.call-update) | async-done | bytes 1048592 | tf_op jit(solution)/shard_map/all_gather | solution.py:13
  52.6 1.3 reduce_sum.18
  54.6 0.8 copy.16
  55.5 181.7 %all-reduce.8.cloned.1.call-done = (f32[256,256]{0,1:T(8,128)}, f32[256,128]{1,0:T(8,128)}) async-done(((f32[256,256]{0,1:T(8,128)}, f32[256,128]{1,0:T(8,128)}), (f32[256,256]{0,1:T(8,128)}, f32[256,128]{1,0:T(8,128)})) %all-reduce.8.cloned.1.call-update) | async-done | bytes 393232 | tf_op jit(solution)/shard_map/psum | solution.py:77
  237.2 1.1 copy.17
  238.2 1.0 fusion.1
  239.3 11.7 %cholesky.130 = f32[128,128]{1,0:T(8,128)S(1)} custom-call(f32[128,128]{1,0:T(8,128)S(1)} %cholesky.194), custom_call_target="Cholesky" | custom-call | tf_op jit(solution)/shard_map/jit(cholesky)/cholesky | solution.py:78
  251.0 9.8 %custom-call.13 = f32[1,128,128]{1,2,0:T(8,128)S(1)} custom-call(f32[1,128,128]{2,1,0:T(8,128)S(1)} %get-tuple-element.61), custom_call_target="InvertDiagBlocksLowerTriangular" | custom-call | tf_op jit(solution)/shard_map/jit(cholesky)/cholesky | solution.py:78
  261.3 11.7 %cholesky.147 = f32[128,128]{1,0:T(8,128)S(1)} custom-call(f32[128,128]{1,0:T(8,128)S(1)} %convolution_subtract_fusion.7), custom_call_target="Cholesky" | custom-call | tf_op jit(solution)/shard_map/jit(cholesky)/cholesky | solution.py:78
  275.8 4.5 while.4
  276.8 1.4 bitcast_dynamic-update-slice_fusion.4
  278.8 1.4 bitcast_dynamic-update-slice_fusion.4
  280.2 19.7 %custom-call.14 = f32[2,128,128]{1,2,0:T(8,128)S(1)} custom-call(f32[2,128,128]{2,1,0:T(8,128)S(1)} %get-tuple-element.26), custom_call_target="InvertDiagBlocksLowerTriangular" | custom-call | tf_op jit(solution)/shard_map/jit(_solve_triangular)/triangular_solve | solution.py:79
  301.3 0.6 constant_dynamic-slice_fusion.3
  302.7 79.1 %all-gather.7.cloned.1.call-done = f32[4096,256]{1,0:T(8,128)} async-done(((f32[64,256]{1,0:T(8,128)}), f32[4096,256]{1,0:T(8,128)}) %all-gather.7.cloned.1.call-update) | async-done | bytes 4194320 | tf_op jit(solution)/shard_map/all_gather | solution.py:86
  381.8 11.4 %convolution_subtract_fusion.1 = f32[256,4096]{1,0:T(8,128)S(1)} fusion(f32[256,4096]{1,0:T(8,128)} %bitcast.110, f32[256,256]{1,0:T(8,128)S(1)} %fusion.10, f32[4096,256]{1,0:T(8,128)} %all-gather.7.cloned.1.call-done), kind=kOutput, calls=%fused_computation.11 | convolution fusion | flops 3222274048 | bytes 12845056 | tf_op jit(solution)/shard_map/dot_general | solution.py:17
  393.2 2.0 copy-done.1
  395.2 0.7 dynamic-slice_select_fusion
  397.8 0.7 copy.25
  398.5 20.2 %all-gather.13.cloned.1.call-done = f32[1024,256]{1,0:T(8,128)} async-done(((f32[256,256]{1,0:T(8,128)}), f32[1024,256]{1,0:T(8,128)}) %all-gather.13.cloned.1.call-update) | async-done | bytes 1048592 | tf_op jit(solution)/shard_map/all_gather | solution.py:13
  418.7 1.3 reduce_sum.19
  420.6 0.8 copy.20
  421.7 181.7 %all-reduce.6.cloned.1.call-done = (f32[256,256]{0,1:T(8,128)}, f32[256,128]{1,0:T(8,128)}) async-done(((f32[256,256]{0,1:T(8,128)}, f32[256,128]{1,0:T(8,128)}), (f32[256,256]{0,1:T(8,128)}, f32[256,128]{1,0:T(8,128)})) %all-reduce.6.cloned.1.call-update) | async-done | bytes 393232 | tf_op jit(solution)/shard_map/psum | solution.py:77
  603.4 1.1 copy.21
  604.5 1.0 fusion
  605.5 11.7 %cholesky.164 = f32[128,128]{1,0:T(8,128)S(1)} custom-call(f32[128,128]{1,0:T(8,128)S(1)} %cholesky.197), custom_call_target="Cholesky" | custom-call | tf_op jit(solution)/shard_map/jit(cholesky)/cholesky | solution.py:78
  617.3 9.8 %custom-call.15 = f32[1,128,128]{1,2,0:T(8,128)S(1)} custom-call(f32[1,128,128]{2,1,0:T(8,128)S(1)} %get-tuple-element.57), custom_call_target="InvertDiagBlocksLowerTriangular" | custom-call | tf_op jit(solution)/shard_map/jit(cholesky)/cholesky | solution.py:78
  627.6 11.7 %cholesky.181 = f32[128,128]{1,0:T(8,128)S(1)} custom-call(f32[128,128]{1,0:T(8,128)S(1)} %convolution_subtract_fusion.6), custom_call_target="Cholesky" | custom-call | tf_op jit(solution)/shard_map/jit(cholesky)/cholesky | solution.py:78
  641.9 4.2 while.5
  642.8 1.4 bitcast_dynamic-update-slice_fusion.5
  644.8 1.4 bitcast_dynamic-update-slice_fusion.5
  646.2 19.7 %custom-call.16 = f32[2,128,128]{1,2,0:T(8,128)S(1)} custom-call(f32[2,128,128]{2,1,0:T(8,128)S(1)} %get-tuple-element.27), custom_call_target="InvertDiagBlocksLowerTriangular" | custom-call | tf_op jit(solution)/shard_map/jit(_solve_triangular)/triangular_solve | solution.py:79
  667.8 0.7 sort.32
  670.8 0.7 pad_maximum_fusion.3
  671.5 0.7 broadcast_select_fusion.2
  672.2 0.9 bitcast_select_fusion
  673.1 74.6 %all-gather.9.cloned.1.call-done = f32[4096,256]{1,0:T(8,128)} async-done(((f32[64,256]{1,0:T(8,128)}), f32[4096,256]{1,0:T(8,128)}) %all-gather.9.cloned.1.call-update) | async-done | bytes 4194320 | tf_op jit(solution)/shard_map/all_gather | solution.py:86
  747.7 12.7 %convolution_subtract_fusion = f32[256,4096]{1,0:T(8,128)} fusion(f32[256,4096]{1,0:T(8,128)} %copy-done.1, f32[256,256]{1,0:T(8,128)S(1)} %fusion.8, f32[4096,256]{1,0:T(8,128)} %all-gather.9.cloned.1.call-done), kind=kOutput, calls=%fused_computation.10 | convolution fusion | flops 3222274048 | bytes 12845056 | tf_op jit(solution)/shard_map/dot_general | solution.py:17
  760.4 4.9 gather_fusion.3
  765.4 4.8 broadcast_select_fusion
  (86 shorter events, 15.3 us)
Async XLA Ops:
  7.2 15.9 %copy-start = (f32[256,128]{1,0:T(8,128)S(1)}, f32[256,128]{1,0:T(8,128)}, u32[]{:S(2)}) copy-start(f32[256,128]{1,0:T(8,128)} %param.14) | copy-start | bytes 393220
  7.2 45.5 %all-gather.11.cloned.1.call-start = ((), (), s32[]{:S(2)}) async-start(), calls=%async_computation.2 | async-start | bytes 1310720 | tf_op jit(solution)/shard_map/all_gather | solution.py:13
  20.3 2.0 copy-start.2
  23.0 214.1 %all-reduce.8.cloned.1.call-start = ((), (), s32[]{:S(2)}) async-start(), calls=%async_computation.5 | async-start | bytes 786432 | tf_op jit(solution)/shard_map/psum | solution.py:77
  55.4 326.4 %all-gather.7.cloned.1.call-start = ((), (), s32[]{:S(2)}) async-start(), calls=%async_computation | async-start | bytes 4259840 | tf_op jit(solution)/shard_map/all_gather | solution.py:86
  301.9 116.7 %all-gather.13.cloned.1.call-start = ((), (), s32[]{:S(2)}) async-start(), calls=%async_computation.3 | async-start | bytes 1310720 | tf_op jit(solution)/shard_map/all_gather | solution.py:13
  302.6 94.0 %copy-start.3 = (f32[256,128]{1,0:T(8,128)S(1)}, f32[256,128]{1,0:T(8,128)}, u32[]{:S(2)}) copy-start(f32[256,128]{1,0:T(8,128)} %get-tuple-element.47) | copy-start | bytes 393220
  393.2 2.0 copy-start.1
  396.0 207.4 %all-reduce.6.cloned.1.call-start = ((), (), s32[]{:S(2)}) async-start(), calls=%async_computation.4 | async-start | bytes 786432 | tf_op jit(solution)/shard_map/psum | solution.py:77
  421.4 326.3 %all-gather.9.cloned.1.call-start = ((), (), s32[]{:S(2)}) async-start(), calls=%async_computation.1 | async-start | bytes 4259840 | tf_op jit(solution)/shard_map/all_gather | solution.py:86
  603.4 65.4 %copy-start.4 = (f32[256,128]{1,0:T(8,128)S(1)}, f32[256,128]{1,0:T(8,128)}, u32[]{:S(2)}) copy-start(f32[256,128]{1,0:T(8,128)} %get-tuple-element.45) | copy-start | bytes 393220
Sparse Core Ops, SparseCore 0:
  23.2 29.4 all-gather.10
  56.7 180.3 all-reduce.7
  302.0 79.6 all-gather.6
  396.1 22.5 all-gather.12
  423.0 180.3 all-reduce.5
  667.9 79.7 all-gather.8
